TPU v7x, 32 devices: a whole 2x2x4 slice. The times are simulated.
32 devices in a mesh: dp: 8 (over z, x), tensor: 4 (over y, core).
Axes of the slice: x: 2, y: 2, z: 4, core: 2. Of those that a mesh axis runs over, the one named last changes fastest.
Arguments:
- tokens_in: bfloat16 [12288, 768], P('dp'), may hold values from -6 to 6
- cotangent: bfloat16 [12288, 768], P('dp'), may hold values from -6 to 6
- span_mask: int32 [12288], P('dp'), may hold values from 0 to 1, as said below
- lengths: int32 [24], P('dp'), may hold values from 128 to 512, as said below
- step: int32 [1], replicated, may hold values from 1000 to 31999
- warmup: int32 [1], replicated, may hold values from 1000 to 29999
- total: int32 [1], replicated, may hold values from 32000 to 40000
- w_qkv: float32 [768, 3, 768], P(None, None, 'tensor'), may hold values from -0.21875 to 0.21875
- w_out: float32 [768, 768], P(None, 'tensor'), may hold values from -1.25 to 1.25
- w_in: float32 [768, 3072], P(None, 'tensor'), may hold values from -0.21875 to 0.21875
- w_back: float32 [768, 3072], P(None, 'tensor'), may hold values from -0.109375 to 0.109375
- gains: float32 [2, 768], replicated, may hold values from 0.5 to 1.5
- biases: float32 [6, 768], replicated, may hold values from -3 to 3
- bias_in: float32 [3072], replicated, may hold values from -3 to 3
- mom_qkv: float32 [2, 768, 3, 768], P(None, 'dp', None, 'tensor'), as said below
- mom_out: float32 [2, 768, 768], P(None, 'dp', 'tensor'), as said below
- mom_in: float32 [2, 768, 3072], P(None, 'dp', 'tensor'), as said below
- mom_back: float32 [2, 768, 3072], P(None, 'dp', 'tensor'), as said below
- mom_gains: float32 [2, 2, 768], replicated, as said below
- mom_biases: float32 [2, 6, 768], replicated, as said below
- mom_bias_in: float32 [2, 3072], replicated, as said below
Outputs:
- normed_out: bfloat16 [12288, 768], P('dp')
- input_grad: float32 [12288, 768], P('dp')
- change_qkv: float32 [768, 3, 768], P(None, None, 'tensor')
- change_out_proj: float32 [768, 768], P(None, 'tensor')
- change_in_proj: float32 [768, 3072], P(None, 'tensor')
- change_back_proj: float32 [768, 3072], P(None, 'tensor')
- change_gains: float32 [2, 768], replicated
- change_biases: float32 [6, 768], replicated
- change_bias_in: float32 [3072], replicated
- new_mom_qkv: float32 [2, 768, 3, 768], P(None, 'dp', None, 'tensor')
- new_mom_out: float32 [2, 768, 768], P(None, 'dp', 'tensor')
- new_mom_in: float32 [2, 768, 3072], P(None, 'dp', 'tensor')
- new_mom_back: float32 [2, 768, 3072], P(None, 'dp', 'tensor')
- new_mom_gains: float32 [2, 2, 768], replicated
- new_mom_biases: float32 [2, 6, 768], replicated
- new_mom_bias_in: float32 [2, 3072], replicated
Inputs may be any that keep to these rules, and one draw needn't show every extreme that they name: `span_mask`: marked positions lie below their sequence's length and form unions of spans of 1 to 10 positions; each sequence has at most 76 of them, and in every draw each of the 3 sequences of some index of dp has exactly 76. `lengths`: a sequence's real tokens stand at its start, the rest is padding. step < total. warmup < total. `mom_qkv`: index 1 of the leading dimension holds positive second moments. `mom_out`: index 1 of the leading dimension holds positive second moments. `mom_in`: index 1 of the leading dimension holds positive second moments. `mom_back`: index 1 of the leading dimension holds positive second moments. `mom_gains`: index 1 of the leading dimension holds positive second moments. `mom_biases`: index 1 of the leading dimension holds positive second moments. `mom_bias_in`: index 1 of the leading dimension holds positive second moments.
All inputs are finite; a program needn't handle non-finite values.
Results may differ from a plain program's by a relative error of at most 0.017.
The roundings to bfloat16 on the way count: a program that leaves them out, or rounds other values in their place, can miss the bound.
Values sent between devices are 32-bit elements; how exact they have to be, the bound alone decides.
A program may use at most 128 MiB of HBM per device.

v0:
```python
import math
import jax
import jax.numpy as jnp
from jax import lax
from jax.sharding import PartitionSpec as P

HD = 64
SPAN_ROWS = 80
NORM_EPS = 1e-12
BETA_ONE = 0.9
BETA_TWO = 0.999
ADAM_EPS = 1e-06
WEIGHT_DECAY = 0.01


def layer_norm(values, gain, shift):
    center = values - jnp.mean(values, axis=-1, keepdims=True)
    spread = jnp.mean(center * center, axis=-1, keepdims=True)
    return center * lax.rsqrt(spread + NORM_EPS) * gain + shift


def exact_gelu(values):
    return jax.nn.gelu(values, approximate=False)


def outer_sum(left, right):
    return jnp.einsum("ta,tb->ab", left, right, preferred_element_type=jnp.float32)


def adam_step(weight, grad, moments, ratio, corr_one, corr_two, decay):
    first = BETA_ONE * moments[0] + (1.0 - BETA_ONE) * grad
    second = BETA_TWO * moments[1] + (1.0 - BETA_TWO) * grad * grad
    update = first / corr_one / (jnp.sqrt(second / corr_two) + ADAM_EPS) + decay * weight
    return (-ratio * update, jnp.stack([first, second]))


def on_device(
    tokens_in,
    cotangent,
    span_mask,
    lengths,
    step,
    warmup,
    total,
    w_qkv,
    w_out,
    w_in,
    w_back,
    gains,
    biases,
    bias_in,
    mom_qkv,
    mom_out,
    mom_in,
    mom_back,
    mom_gains,
    mom_biases,
    mom_bias_in,
):
    row_count, model_width = tokens_in.shape
    seq_count = lengths.shape[0]
    seq_length = row_count // seq_count
    head_cols = w_qkv.shape[2]
    hidden_cols = w_in.shape[1]
    head_size = HD
    local_heads = head_cols // head_size
    query_scale = 1.0 / math.sqrt(head_size)
    tensor_slot = lax.axis_index("tensor")
    bias_query = lax.dynamic_slice_in_dim(biases[0], tensor_slot * head_cols, head_cols)
    bias_value = lax.dynamic_slice_in_dim(biases[1], tensor_slot * head_cols, head_cols)
    bias_hidden = lax.dynamic_slice_in_dim(bias_in, tensor_slot * hidden_cols, hidden_cols)
    qkv_low = w_qkv.astype(jnp.bfloat16).reshape(model_width, 3 * head_cols)
    out_low = w_out.astype(jnp.bfloat16)
    in_low = w_in.astype(jnp.bfloat16)
    down_low = w_back.astype(jnp.bfloat16)
    projected = jnp.dot(tokens_in, qkv_low, preferred_element_type=jnp.float32).reshape(
        row_count, 3, head_cols
    )
    attn_shape = (seq_count, seq_length, local_heads, head_size)
    queries = (
        ((projected[:, 0] + bias_query) * query_scale).astype(jnp.bfloat16).reshape(attn_shape)
    )
    keys = projected[:, 1].astype(jnp.bfloat16).reshape(attn_shape)
    values = (projected[:, 2] + bias_value).astype(jnp.bfloat16).reshape(attn_shape)
    positions = jnp.arange(seq_length, dtype=jnp.int32)
    inside = positions[None, :] < lengths[:, None]
    key_bias = jnp.where(inside, 0.0, -1000000000.0).astype(jnp.float32)

    def score_block():
        raw = jnp.einsum("sqhd,skhd->shqk", queries, keys, preferred_element_type=jnp.float32)
        return raw + key_bias[:, None, None, :]

    scores = score_block()
    peak = jnp.max(scores, axis=-1, keepdims=True)
    log_total = peak + jnp.log(jnp.sum(jnp.exp(scores - peak), axis=-1, keepdims=True))
    probs_low = jnp.exp(scores - log_total).astype(jnp.bfloat16)
    context_low = (
        jnp.einsum("shqk,skhd->sqhd", probs_low, values, preferred_element_type=jnp.float32)
        .reshape(row_count, head_cols)
        .astype(jnp.bfloat16)
    )
    attn_part = jnp.einsum("tc,dc->td", context_low, out_low, preferred_element_type=jnp.float32)
    attn_sum = lax.psum(attn_part, "tensor")
    residual_one = tokens_in.astype(jnp.float32) + attn_sum + biases[2]
    normed = layer_norm(residual_one, gains[0], biases[3])
    normed_low = normed.astype(jnp.bfloat16)
    pre_act = jnp.dot(normed_low, in_low, preferred_element_type=jnp.float32) + bias_hidden
    act_low = exact_gelu(pre_act).astype(jnp.bfloat16)
    down_part = jnp.einsum("tf,df->td", act_low, down_low, preferred_element_type=jnp.float32)
    down_sum = lax.psum(down_part, "tensor")
    residual_two = normed + down_sum + biases[4]
    live = inside.astype(jnp.int32) * span_mask.reshape(seq_count, seq_length) > 0
    upto = (positions[:, None] <= positions[None, :]).astype(jnp.float32)
    rank = jnp.dot(live.astype(jnp.float32), upto).astype(jnp.int32) - 1
    slots = jnp.arange(SPAN_ROWS, dtype=jnp.int32)
    pick = (live[:, None, :] & (rank[:, None, :] == slots[None, :, None])).astype(jnp.float32)
    pick_low = pick.astype(jnp.bfloat16)

    def rows_of(values):
        width = values.shape[-1]
        return jnp.einsum(
            "srt,std->srd",
            pick,
            values.reshape(seq_count, seq_length, width),
            precision=lax.Precision.HIGHEST,
        ).reshape(seq_count * SPAN_ROWS, width)

    def low_rows_of(values):
        width = values.shape[-1]
        return jnp.einsum(
            "srt,std->srd",
            pick_low,
            values.reshape(seq_count, seq_length, width),
            preferred_element_type=jnp.bfloat16,
        ).reshape(seq_count * SPAN_ROWS, width)

    result = layer_norm(residual_two, gains[1], biases[5])
    normed_out = result.astype(jnp.bfloat16)
    residual_one_rows = rows_of(residual_one)
    residual_two_rows = rows_of(residual_two)
    grad_result = low_rows_of(cotangent).astype(jnp.float32)
    _, norm_two_back = jax.vjp(layer_norm, residual_two_rows, gains[1], biases[5])
    d_res_two, d_gain_two, d_shift_two = norm_two_back(grad_result)
    d_res_two_low = d_res_two.astype(jnp.bfloat16)
    normed_low_rows = low_rows_of(normed_low)
    pre_rows = jnp.dot(normed_low_rows, in_low, preferred_element_type=jnp.float32) + bias_hidden
    act_rows, gelu_back = jax.vjp(exact_gelu, pre_rows)
    grad_back = outer_sum(d_res_two_low, act_rows.astype(jnp.bfloat16))
    d_act = jnp.dot(d_res_two_low, down_low, preferred_element_type=jnp.float32)
    d_pre = gelu_back(d_act)[0]
    d_pre_low = d_pre.astype(jnp.bfloat16)
    grad_in = outer_sum(normed_low_rows, d_pre_low)
    d_normed_part = jnp.einsum("tf,df->td", d_pre_low, in_low, preferred_element_type=jnp.float32)
    d_normed = lax.psum(d_normed_part, "tensor") + d_res_two
    _, norm_one_back = jax.vjp(layer_norm, residual_one_rows, gains[0], biases[3])
    d_res_one, d_gain_one, d_shift_one = norm_one_back(d_normed)
    d_res_one_low = d_res_one.astype(jnp.bfloat16)
    grad_out_proj = outer_sum(d_res_one_low, low_rows_of(context_low))
    row_shape = (seq_count, SPAN_ROWS, local_heads, head_size)
    d_context = (
        jnp.dot(d_res_one_low, out_low, preferred_element_type=jnp.float32)
        .astype(jnp.bfloat16)
        .reshape(row_shape)
    )
    query_rows = low_rows_of(queries.reshape(row_count, head_cols)).reshape(row_shape)
    raw = jnp.einsum("sqhd,skhd->shqk", query_rows, keys, preferred_element_type=jnp.float32)
    probs = jax.nn.softmax(raw + key_bias[:, None, None, :], axis=-1)
    probs_again = probs.astype(jnp.bfloat16)
    d_probs = jnp.einsum("sqhd,skhd->shqk", d_context, values, preferred_element_type=jnp.float32)
    d_values = jnp.einsum(
        "shqk,sqhd->skhd", probs_again, d_context, preferred_element_type=jnp.float32
    ).reshape(row_count, head_cols)
    d_scores = (probs * (d_probs - jnp.sum(probs * d_probs, axis=-1, keepdims=True))).astype(
        jnp.bfloat16
    )
    d_queries = (
        jnp.einsum("shqk,skhd->sqhd", d_scores, keys, preferred_element_type=jnp.float32).reshape(
            seq_count * SPAN_ROWS, head_cols
        )
        * query_scale
    )
    d_keys = jnp.einsum(
        "shqk,sqhd->skhd", d_scores, query_rows, preferred_element_type=jnp.float32
    ).reshape(row_count, head_cols)

    def spread(row_values):
        width = row_values.shape[-1]
        return jnp.einsum(
            "srt,srd->std",
            pick,
            row_values.reshape(seq_count, SPAN_ROWS, width),
            precision=lax.Precision.HIGHEST,
        ).reshape(row_count, width)

    d_proj_low = (
        jnp.stack([spread(d_queries), d_keys, d_values], axis=1)
        .astype(jnp.bfloat16)
        .reshape(row_count, 3 * head_cols)
    )
    grad_qkv = outer_sum(tokens_in, d_proj_low).reshape(model_width, 3, head_cols)
    d_entry_part = jnp.einsum("tc,dc->td", d_proj_low, qkv_low, preferred_element_type=jnp.float32)
    input_grad = lax.psum(d_entry_part, "tensor") + spread(d_res_one)
    first_rank = (tensor_slot == 0).astype(jnp.float32)
    width_zero = jnp.zeros((model_width,), jnp.float32)

    def place_heads(partial_sum):
        return lax.dynamic_update_slice_in_dim(width_zero, partial_sum, tensor_slot * head_cols, 0)

    grad_gains = jnp.stack([d_gain_one, d_gain_two]) * first_rank
    grad_biases = jnp.stack(
        [
            place_heads(jnp.sum(d_queries, axis=0)),
            place_heads(jnp.sum(d_values, axis=0)),
            jnp.sum(d_res_one, axis=0) * first_rank,
            d_shift_one * first_rank,
            jnp.sum(d_res_two, axis=0) * first_rank,
            d_shift_two * first_rank,
        ]
    )
    grad_bias_in = lax.dynamic_update_slice_in_dim(
        jnp.zeros(bias_in.shape, jnp.float32), jnp.sum(d_pre, axis=0), tensor_slot * hidden_cols, 0
    )
    grad_gains, grad_biases, grad_bias_in = lax.psum(
        (grad_gains, grad_biases, grad_bias_in), ("dp", "tensor")
    )
    data_slot = lax.axis_index("dp")
    shard_rows = model_width // lax.axis_size("dp")
    owned = tuple(
        (
            lax.psum_scatter(part, "dp", scatter_dimension=0, tiled=True)
            for part in (grad_qkv, grad_out_proj, grad_in, grad_back)
        )
    )
    clock = step[0].astype(jnp.float32)
    warm = warmup[0].astype(jnp.float32)
    horizon = total[0].astype(jnp.float32)
    ratio = jnp.minimum(clock / warm, (horizon - clock) / (horizon - warm))
    corr_one = 1.0 - jnp.power(BETA_ONE, clock)
    corr_two = 1.0 - jnp.power(BETA_TWO, clock)
    change_rows = []
    fresh_moments = []
    for weight, grad_rows, moment in zip(
        (w_qkv, w_out, w_in, w_back), owned, (mom_qkv, mom_out, mom_in, mom_back)
    ):
        weight_rows = lax.dynamic_slice_in_dim(weight, data_slot * shard_rows, shard_rows, 0)
        row_change, new_moment = adam_step(
            weight_rows, grad_rows, moment, ratio, corr_one, corr_two, WEIGHT_DECAY
        )
        change_rows.append(row_change)
        fresh_moments.append(new_moment)
    change_qkv, change_out_proj, change_in_proj, change_back_proj = (
        lax.all_gather(change_rows[0], "dp", axis=0, tiled=True),
        lax.all_gather(change_rows[1], "dp", axis=0, tiled=True),
        lax.all_gather(change_rows[2], "dp", axis=0, tiled=True),
        lax.all_gather(change_rows[3], "dp", axis=0, tiled=True),
    )
    change_gains, new_mom_gains = adam_step(
        gains, grad_gains, mom_gains, ratio, corr_one, corr_two, 0.0
    )
    change_biases, new_mom_biases = adam_step(
        biases, grad_biases, mom_biases, ratio, corr_one, corr_two, 0.0
    )
    change_bias_in, new_mom_bias_in = adam_step(
        bias_in, grad_bias_in, mom_bias_in, ratio, corr_one, corr_two, 0.0
    )
    return (
        normed_out,
        input_grad,
        change_qkv,
        change_out_proj,
        change_in_proj,
        change_back_proj,
        change_gains,
        change_biases,
        change_bias_in,
        fresh_moments[0],
        fresh_moments[1],
        fresh_moments[2],
        fresh_moments[3],
        new_mom_gains,
        new_mom_biases,
        new_mom_bias_in,
    )


def solution(mesh):
    in_specs = (
        P("dp", None),
        P("dp", None),
        P("dp"),
        P("dp"),
        P(),
        P(),
        P(),
        P(None, None, "tensor"),
        P(None, "tensor"),
        P(None, "tensor"),
        P(None, "tensor"),
        P(),
        P(),
        P(),
        P(None, "dp", None, "tensor"),
        P(None, "dp", "tensor"),
        P(None, "dp", "tensor"),
        P(None, "dp", "tensor"),
        P(),
        P(),
        P(),
    )
    out_specs = (
        P("dp", None),
        P("dp", None),
        P(None, None, "tensor"),
        P(None, "tensor"),
        P(None, "tensor"),
        P(None, "tensor"),
        P(),
        P(),
        P(),
        P(None, "dp", None, "tensor"),
        P(None, "dp", "tensor"),
        P(None, "dp", "tensor"),
        P(None, "dp", "tensor"),
        P(),
        P(),
        P(),
    )
    return jax.shard_map(
        on_device, mesh=mesh, in_specs=in_specs, out_specs=out_specs, check_vma=False
    )
```

profile of v0, /device:TPU:0, one launch (start us, length us, event | category | flops | bytes accessed | tf_op | source)
XLA Modules:
  0.0 894.0 jit_solution(5073173420024962855)
XLA Ops:
  7.2 3.9 fusion.15
  13.9 2.1 convert_element_type.129
  18.3 1.8 fusion.168
  22.7 2.8 add_reduce_fusion
  27.3 1.8 copy-done.3
  29.8 2.8 squeeze.6
  34.5 5.7 fusion.20
  41.2 3.0 fusion.96
  46.6 94.5 %all-reduce.6.cloned.1.call-done = f32[1536,768]{1,0:T(8,128)} async-done(((f32[1536,768]{1,0:T(8,128)}), f32[1536,768]{1,0:T(8,128)}) %all-reduce.6.cloned.1.call-update) | async-done | bytes 4718608 | tf_op jit(solution)/shard_map/psum | solution.py:103
  141.1 3.8 fusion.167
  147.1 2.1 fusion.14
  149.2 17.8 %fusion.18 = f32[1536,768]{1,0:T(8,128)} fusion(bf16[1536,768]{1,0:T(8,128)(2,1)} %fusion.14, f32[768]{0:T(1024)} %dynamic_slice.23, f32[768,768]{1,0:T(8,128)} %param.31, f32[768,768]{1,0:T(8,128)} %param.30), kind=kOutput, calls=%fused_computation.39 | convolution fusion | flops 3702915072 | bytes 11799552 | tf_op jit(solution)/shard_map/tf,df->td/dot_general | solution.py:109
  170.6 2.0 fusion.35
  172.6 3.1 fusion.175
  175.7 4.6 fusion.173
  183.3 78.0 %all-reduce.8.cloned.1.call-done = f32[1536,768]{1,0:T(8,128)} async-done(((f32[1536,768]{1,0:T(8,128)}), f32[1536,768]{1,0:T(8,128)}) %all-reduce.8.cloned.1.call-update) | async-done | bytes 4718608 | tf_op jit(solution)/shard_map/psum | solution.py:110
  261.3 5.3 fusion.166
  266.7 2.2 copy-done.4
  268.9 2.1 fusion.174
  271.0 2.0 multiply_reduce_fusion.8
  276.3 4.8 fusion.180
  283.3 33.8 %all-reduce.10.cloned.1.call-done = f32[240,768]{1,0:T(8,128)} async-done(((f32[240,768]{1,0:T(8,128)}), f32[240,768]{1,0:T(8,128)}) %all-reduce.10.cloned.1.call-update) | async-done | bytes 737296 | tf_op jit(solution)/shard_map/psum | solution.py:154
  317.0 2.2 fusion.163
  323.2 2.6 fusion.179
  339.3 4.4 fusion.181
  343.7 3.0 copy.97
  346.8 1.9 fusion.89
  348.8 4.6 fusion.62
  355.3 6.1 convolution_bitcast_fusion
  365.0 51.3 %reduce-scatter.5.cloned.1.call-done = f32[96,3,192]{2,0,1:T(8,128)} async-done(((f32[768,3,192]{2,0,1:T(8,128)}), f32[96,3,192]{2,0,1:T(8,128)}) %reduce-scatter.5.cloned.1.call-update) | async-done | bytes 221200 | tf_op jit(solution)/shard_map/reduce_scatter | solution.py:230
  416.3 2.2 fusion.104
  418.5 69.8 %reduce-scatter.9.cloned.1.call-done = f32[96,768]{1,0:T(8,128)} async-done(((f32[768,768]{1,0:T(8,128)}), f32[96,768]{1,0:T(8,128)}) %reduce-scatter.9.cloned.1.call-update) | async-done | bytes 294928 | tf_op jit(solution)/shard_map/reduce_scatter | solution.py:230
  488.3 2.2 fusion.105
  492.8 3.0 multiply_reduce_fusion
  495.9 4.2 add_convert_fusion
  500.1 59.7 %reduce-scatter.11.cloned.1.call-done = f32[96,768]{1,0:T(8,128)} async-done(((f32[768,768]{1,0:T(8,128)}), f32[96,768]{1,0:T(8,128)}) %reduce-scatter.11.cloned.1.call-update) | async-done | bytes 294928 | tf_op jit(solution)/shard_map/reduce_scatter | solution.py:230
  559.9 2.0 fusion.106
  562.9 40.3 %all-reduce = (f32[2,768]{1,0:T(2,128)S(1)}, f32[6,768]{1,0:T(8,128)S(1)}, f32[3072]{0:T(1024)S(1)}) all-reduce(f32[2,768]{1,0:T(2,128)S(1)} %maximum_multiply_fusion, f32[6,768]{1,0:T(8,128)S(1)} %stack.88, f32[3072]{0:T(1024)S(1)} %dynamic_update_slice.13), channel_id=1, replica_groups=mesh['dp'=8,'tensor'=4] {'dp','tensor'}, use_global_device_ids=true, to_apply=%region_27.28 | all-reduce | flops 9216 | bytes 73728 | tf_op jit(solution)/shard_map/psum | solution.py:223
  607.0 4.3 fusion.47
  611.3 13.9 %reduce-scatter.7.cloned.1.call-done = f32[96,192]{1,0:T(8,128)} async-done(((f32[768,192]{1,0:T(8,128)}), f32[96,192]{1,0:T(8,128)}) %reduce-scatter.7.cloned.1.call-update) | async-done | bytes 73744 | tf_op jit(solution)/shard_map/reduce_scatter | solution.py:230
  626.3 32.2 %all_gather.13 = f32[768,192]{1,0:T(8,128)S(1)} all-gather(f32[96,192]{1,0:T(8,128)S(1)} %get-tuple-element.107), channel_id=1, replica_groups=mesh['dp'=8,'tensor'=4] {'dp'}, dimensions={0}, use_global_device_ids=true | all-gather | bytes 663552 | tf_op jit(solution)/shard_map/all_gather | solution.py:253
  660.3 60.5 %all-reduce.12.cloned.1.call-done = f32[1536,768]{1,0:T(8,128)} async-done(((f32[1536,768]{1,0:T(8,128)}), f32[1536,768]{1,0:T(8,128)}) %all-reduce.12.cloned.1.call-update) | async-done | bytes 4718608 | tf_op jit(solution)/shard_map/psum | solution.py:202
  720.8 6.6 bitcast_add_fusion
  729.9 46.0 %all-gather.4.cloned.1.call-done = f32[768,3,192]{2,0,1:T(8,128)} async-done(((f32[96,3,192]{2,0,1:T(8,128)}), f32[768,3,192]{2,0,1:T(8,128)}) %all-gather.4.cloned.1.call-update) | async-done | bytes 1769488 | tf_op jit(solution)/shard_map/all_gather | solution.py:252
  775.9 2.9 copy.102
  778.8 50.6 %all-gather.6.cloned.1.call-done = f32[768,768]{1,0:T(8,128)} async-done(((f32[96,768]{1,0:T(8,128)}), f32[768,768]{1,0:T(8,128)}) %all-gather.6.cloned.1.call-update) | async-done | bytes 2359312 | tf_op jit(solution)/shard_map/all_gather | solution.py:254
  829.4 53.1 %all-gather.8.cloned.1.call-done = f32[768,768]{1,0:T(8,128)} async-done(((f32[96,768]{1,0:T(8,128)}), f32[768,768]{1,0:T(8,128)}) %all-gather.8.cloned.1.call-update) | async-done | bytes 2359312 | tf_op jit(solution)/shard_map/all_gather | solution.py:255
  882.5 3.4 copy.181
  (253 shorter events, 64.1 us)
Async XLA Ops:
  7.2 263.8 %copy-start = (bf16[1536,768]{1,0:T(8,128)(2,1)S(1)}, bf16[1536,768]{1,0:T(8,128)(2,1)}, u32[]{:S(2)}) copy-start(bf16[1536,768]{1,0:T(8,128)(2,1)} %param.22) | copy-start | bytes 7077892
  7.2 133.9 %all-reduce.6.cloned.1.call-start = ((), (), s32[]{:S(2)}) async-start(), calls=%async_computation.4 | async-start | bytes 9437184 | tf_op jit(solution)/shard_map/psum | solution.py:103
  25.5 7.0 copy-start.60
  34.4 6.7 copy-start.19
  44.2 217.1 %all-reduce.8.cloned.1.call-start = ((), (), s32[]{:S(2)}) async-start(), calls=%async_computation.5 | async-start | bytes 9437184 | tf_op jit(solution)/shard_map/psum | solution.py:110
  167.0 150.0 %all-reduce.10.cloned.1.call-start = ((), (), s32[]{:S(2)}) async-start(), calls=%async_computation.6 | async-start | bytes 1474560 | tf_op jit(solution)/shard_map/psum | solution.py:154
  172.6 9.3 %copy-start.26 = (bf16[3,80,192]{1,2,0:T(8,128)(2,1)}, bf16[3,80,192]{1,2,0:T(8,128)(2,1)S(1)}, u32[]{:S(2)}) copy-start(bf16[3,80,192]{1,2,0:T(8,128)(2,1)S(1)} %fusion.35) | copy-start | bytes 276484
  175.7 6.2 copy-start.8
  175.7 6.2 copy-start.55
  180.3 81.0 %copy-start.31 = (f32[1536]{0:T(1024)S(1)}, f32[1536]{0:T(1024)}, u32[]{:S(2)}) copy-start(f32[1536]{0:T(1024)} %copy-done.30) | copy-start | bytes 18436
  180.3 81.0 %copy-start.35 = (f32[1536]{0:T(1024)S(1)}, f32[1536]{0:T(1024)}, u32[]{:S(2)}) copy-start(f32[1536]{0:T(1024)} %copy-done.34) | copy-start | bytes 18436
  180.3 81.0 %copy-start.40 = (f32[768]{0:T(1024)S(1)}, f32[768]{0:T(1024)}, u32[]{:S(2)}) copy-start(f32[768]{0:T(1024)} %get-tuple-element.118) | copy-start | bytes 9220
  180.3 81.0 %copy-start.57 = (f32[768]{0:T(1024)S(1)}, f32[768]{0:T(1024)}, u32[]{:S(2)}) copy-start(f32[768]{0:T(1024)} %get-tuple-element.119) | copy-start | bytes 9220
  273.2 7.9 copy-start.45
  273.2 7.9 copy-start.47
  274.6 6.4 copy-start.49
  282.5 133.8 %reduce-scatter.5.cloned.1.call-start = ((), (), s32[]{:S(2)}) async-start(), calls=%async_computation.8 | async-start | bytes 2654208 | tf_op jit(solution)/shard_map/reduce_scatter | solution.py:230
  330.9 8.4 copy-start.21
  346.7 141.6 %reduce-scatter.9.cloned.1.call-start = ((), (), s32[]{:S(2)}) async-start(), calls=%async_computation.11 | async-start | bytes 2654208 | tf_op jit(solution)/shard_map/reduce_scatter | solution.py:230
  348.8 211.1 %reduce-scatter.11.cloned.1.call-start = ((), (), s32[]{:S(2)}) async-start(), calls=%async_computation.13 | async-start | bytes 2654208 | tf_op jit(solution)/shard_map/reduce_scatter | solution.py:230
  353.4 271.8 %reduce-scatter.7.cloned.1.call-start = ((), (), s32[]{:S(2)}) async-start(), calls=%async_computation.10 | async-start | bytes 884736 | tf_op jit(solution)/shard_map/reduce_scatter | solution.py:230
  355.0 365.8 %all-reduce.12.cloned.1.call-start = ((), (), s32[]{:S(2)}) async-start(), calls=%async_computation.7 | async-start | bytes 9437184 | tf_op jit(solution)/shard_map/psum | solution.py:202
  361.3 130.4 %copy-start.38 = (f32[2,6,768]{2,0,1:T(2,128)S(1)}, f32[2,6,768]{2,0,1:T(2,128)}, u32[]{:S(2)}) copy-start(f32[2,6,768]{2,0,1:T(2,128)} %param.40) | copy-start | bytes 110596
  361.3 130.4 %copy-start.42 = (f32[2,3072]{1,0:T(2,128)S(1)}, f32[2,3072]{1,0:T(2,128)}, u32[]{:S(2)}) copy-start(f32[2,3072]{1,0:T(2,128)} %param.41) | copy-start | bytes 73732
  361.3 131.0 %copy-start.7 = (f32[3,80,768]{2,1,0:T(8,128)S(1)}, f32[3,80,768]{2,1,0:T(8,128)}, u32[]{:S(2)}) copy-start(f32[3,80,768]{2,1,0:T(8,128)} %get-tuple-element.137) | copy-start | bytes 2211844
  361.3 131.0 %copy-start.46 = (f32[3,80]{1,0:T(4,128)S(1)}, f32[3,80]{1,0:T(4,128)}, u32[]{:S(2)}) copy-start(f32[3,80]{1,0:T(4,128)} %copy-done.45) | copy-start | bytes 2884
  361.3 131.0 %copy-start.48 = (f32[3,80]{1,0:T(4,128)S(1)}, f32[3,80]{1,0:T(4,128)}, u32[]{:S(2)}) copy-start(f32[3,80]{1,0:T(4,128)} %copy-done.47) | copy-start | bytes 2884
  361.3 131.0 %copy-start.50 = (f32[3,80]{1,0:T(4,128)S(1)}, f32[3,80]{1,0:T(4,128)}, u32[]{:S(2)}) copy-start(f32[3,80]{1,0:T(4,128)} %copy-done.49) | copy-start | bytes 2884
  361.4 131.4 %copy-start.41 = (f32[1536]{0:T(1024)S(1)}, f32[1536]{0:T(1024)}, u32[]{:S(2)}) copy-start(f32[1536]{0:T(1024)} %get-tuple-element.88) | copy-start | bytes 18436
  361.4 414.5 %all-gather.4.cloned.1.call-start = ((), (), s32[]{:S(2)}) async-start(), calls=%async_computation.9 | async-start | bytes 2654208 | tf_op jit(solution)/shard_map/all_gather | solution.py:252
  418.4 77.3 %copy-start.51 = (f32[768]{0:T(1024)S(1)}, f32[768]{0:T(1024)}, u32[]{:S(2)}) copy-start(f32[768]{0:T(1024)} %get-tuple-element.120) | copy-start | bytes 9220
  418.5 410.9 %all-gather.6.cloned.1.call-start = ((), (), s32[]{:S(2)}) async-start(), calls=%async_computation.12 | async-start | bytes 2654208 | tf_op jit(solution)/shard_map/all_gather | solution.py:254
  490.5 392.0 %all-gather.8.cloned.1.call-start = ((), (), s32[]{:S(2)}) async-start(), calls=%async_computation.14 | async-start | bytes 2654208 | tf_op jit(solution)/shard_map/all_gather | solution.py:255
  495.7 64.1 %copy-start.28 = (f32[2,96,768]{2,1,0:T(8,128)S(1)}, f32[2,96,768]{2,1,0:T(8,128)}, u32[]{:S(2)}) copy-start(f32[2,96,768]{2,1,0:T(8,128)} %param.38) | copy-start | bytes 1769476
  495.8 66.1 %copy-start.56 = (f32[768]{0:T(1024)S(1)}, f32[768]{0:T(1024)}, u32[]{:S(2)}) copy-start(f32[768]{0:T(1024)} %get-tuple-element.70) | copy-start | bytes 9220
  495.8 66.2 %copy-start.59 = (f32[768]{0:T(1024)S(1)}, f32[768]{0:T(1024)}, u32[]{:S(2)}) copy-start(f32[768]{0:T(1024)} %get-tuple-element.146) | copy-start | bytes 9220
  495.8 66.5 %copy-start.52 = (f32[768]{0:T(1024)S(1)}, f32[768]{0:T(1024)}, u32[]{:S(2)}) copy-start(f32[768]{0:T(1024)} %get-tuple-element.66) | copy-start | bytes 9220
  495.8 66.5 %copy-start.62 = (f32[3,64]{1,0:T(4,128)S(1)}, f32[3,64]{1,0:T(4,128)}, u32[]{:S(2)}) copy-start(f32[3,64]{1,0:T(4,128)} %get-tuple-element.142) | copy-start | bytes 2308
  495.8 66.5 %copy-start.61 = (f32[3,64]{1,0:T(4,128)S(1)}, f32[3,64]{1,0:T(4,128)}, u32[]{:S(2)}) copy-start(f32[3,64]{1,0:T(4,128)} %get-tuple-element.144) | copy-start | bytes 2308
  495.8 66.6 %copy-start.54 = (f32[768]{0:T(1024)S(1)}, f32[768]{0:T(1024)}, u32[]{:S(2)}) copy-start(f32[768]{0:T(1024)} %get-tuple-element.85) | copy-start | bytes 9220
  495.8 66.6 %copy-start.53 = (f32[768]{0:T(1024)S(1)}, f32[768]{0:T(1024)}, u32[]{:S(2)}) copy-start(f32[768]{0:T(1024)} %get-tuple-element.71) | copy-start | bytes 9220
  495.9 107.4 %copy-start.33 = (f32[6,768]{1,0:T(8,128)S(1)}, f32[6,768]{1,0:T(8,128)}, u32[]{:S(2)}) copy-start(f32[6,768]{1,0:T(8,128)} %param.33) | copy-start | bytes 55300
  495.9 108.7 %copy-start.43 = (f32[2,768]{1,0:T(2,128)S(1)}, f32[2,768]{1,0:T(2,128)}, u32[]{:S(2)}) copy-start(f32[2,768]{1,0:T(2,128)} %param.32) | copy-start | bytes 18436
  495.9 108.7 %copy-start.58 = (f32[2,2,768]{2,1,0:T(2,128)S(1)}, f32[2,2,768]{2,1,0:T(2,128)}, u32[]{:S(2)}) copy-start(f32[2,2,768]{2,1,0:T(2,128)} %param.39) | copy-start | bytes 36868
  495.9 109.9 %copy-start.36 = (f32[1,3072]{1,0:T(1,128)S(1)}, f32[1,3072]{1,0:T(1,128)}, u32[]{:S(2)}) copy-start(f32[1,3072]{1,0:T(1,128)} %get-tuple-element.113) | copy-start | bytes 36868
  495.9 109.9 %copy-start.37 = (f32[1,3072]{1,0:T(1,128)S(1)}, f32[1,3072]{1,0:T(1,128)}, u32[]{:S(2)}) copy-start(f32[1,3072]{1,0:T(1,128)} %get-tuple-element.114) | copy-start | bytes 36868
  495.9 109.9 %copy-start.44 = (f32[3072]{0:T(1024)S(1)}, f32[3072]{0:T(1024)}, u32[]{:S(2)}) copy-start(f32[3072]{0:T(1024)} %param.34) | copy-start | bytes 36868
  660.3 67.1 %copy-start.25 = (f32[1,96,3,192]{3,1,2,0:T(8,128)S(1)}, f32[1,96,3,192]{3,1,2,0:T(8,128)}, u32[]{:S(2)}) copy-start(f32[1,96,3,192]{3,1,2,0:T(8,128)} %get-tuple-element.103) | copy-start | bytes 663556
  (27 other events, 78.4 us)
Sparse Core Ops, SparseCore 0:
  44.3 96.7 all-reduce.5
  167.1 94.1 all-reduce.7
  282.6 34.3 all-reduce.9
  346.9 69.3 reduce-scatter.4
  420.2 68.0 reduce-scatter.8
  491.6 68.1 reduce-scatter.10
  563.7 61.4 reduce-scatter.6
  627.8 92.9 all-reduce.11
  723.8 52.0 all-gather.3
  778.8 50.5 all-gather.5
  831.8 50.5 all-gather.7
where the time goes:
time: 903 us; the launch traced here: 894 us
  waiting for transfers between devices  611 us (68%)
  matrix products  86.9 us (10%)
  blocking collectives  72.5 us (8%)
  other arithmetic  56.1 us (6%)
  local copies, waits for them, and re-layouts  48.5 us (5%)
  between operations  17.2 us (2%)
    reduce_scatter x4, waiting for transfers between devices, on_device(): lax.psum_scatter(part, 'dp', scatter_dimension=0, tiled=True)  195 us
    psum x1, waiting for transfers between devices, on_device(): attn_sum = lax.psum(attn_part, 'tensor')  94.5 us
    psum x1, waiting for transfers between devices, on_device(): down_sum = lax.psum(down_part, 'tensor')  78 us
    psum x1, waiting for transfers between devices, on_device(): input_grad = lax.psum(d_entry_part, 'tensor') + spread(d_res_one)  60.5 us
    all_gather x1, waiting for transfers between devices, on_device(): lax.all_gather(change_rows[3], 'dp', axis=0, tiled=True)  53.1 us
    all_gather x1, waiting for transfers between devices, on_device(): lax.all_gather(change_rows[2], 'dp', axis=0, tiled=True)  50.6 us
    all_gather x1, waiting for transfers between devices, on_device(): lax.all_gather(change_rows[0], 'dp', axis=0, tiled=True)  46 us
    psum x1, blocking collectives, on_device(): lax.psum((grad_gains, grad_biases, grad_bias_in), ('dp', 'tensor'))  40.3 us
  transfers between devices with their start and end apart: 11, of which 11 were waited for; matrix products, arithmetic and copies ran while one was open for 8% of the time, Pallas kernels for 0%

commit v1 on v0

--- a/solution.py
+++ b/solution.py
@@ -11,6 +11,13 @@
 BETA_TWO = 0.999
 ADAM_EPS = 1e-06
 WEIGHT_DECAY = 0.01
+
+
+def place_flows(z, axis_k):
+    b_now = list(z.shape[1:])
+    b_now[axis_k] *= z.shape[0]
+    v1 = jnp.moveaxis(z, 0, axis_k).reshape(b_now)
+    return v1
 
 
 def layer_norm(values, gain, shift):
@@ -248,8 +255,33 @@
         )
         change_rows.append(row_change)
         fresh_moments.append(new_moment)
+
+    def match_spans(local_values, along_axis, dim_k):
+        by_rank = []
+        n_shards = lax.psum(1, along_axis)
+        for num in tuple(range(n_shards)):
+            by_rank.append((num, (num + 1) % n_shards))
+        gallery = []
+        for ii, j0 in by_rank:
+            gallery.append((j0, ii))
+        reply, later = ([], [])
+        for at in tuple(range(n_shards - 1)):
+            if at % 2 == 0:
+                reply.append(
+                    lax.ppermute(reply[-1] if reply else local_values, along_axis, by_rank)
+                )
+            else:
+                later.append(
+                    lax.ppermute(later[-1] if later else local_values, along_axis, gallery)
+                )
+        row_out = jnp.stack([*reply[::-1], local_values, *later], 0)
+        w_next = lax.axis_index(along_axis) - len(reply)
+        row_out = row_out[(jnp.arange(n_shards) - w_next) % n_shards]
+        piece_out = place_flows(row_out, dim_k)
+        return piece_out
+
     change_qkv, change_out_proj, change_in_proj, change_back_proj = (
-        lax.all_gather(change_rows[0], "dp", axis=0, tiled=True),
+        match_spans(change_rows[0], "dp", 0),
         lax.all_gather(change_rows[1], "dp", axis=0, tiled=True),
         lax.all_gather(change_rows[2], "dp", axis=0, tiled=True),
         lax.all_gather(change_rows[3], "dp", axis=0, tiled=True),

time: 903 us -> 833 us (0.922)
  waiting for transfers between devices: 611 us -> 512 us
  local copies, waits for them, and re-layouts: 48.5 us -> 61.8 us
  starting transfers between devices: 1.42 us -> 11.4 us
    all_gather x1 -> x0, waiting for transfers between devices: 46 us -> none  [on_device(): lax.all_gather(change_rows[0], 'dp', axis=0, tiled=True)]
    all_gather x1, waiting for transfers between devices: 50.6 us -> 20.2 us  [on_device(): lax.all_gather(change_rows[2], 'dp', axis=0, tiled=True)]
    psum x1, waiting for transfers between devices: 33.8 us -> 15.6 us  [on_device(): d_normed = lax.psum(d_normed_part, 'tensor') + d_res_two]
    reduce_scatter x4, waiting for transfers between devices: 195 us -> 177 us  [on_device(): lax.psum_scatter(part, 'dp', scatter_dimension=0, tiled=True)]
    ppermute x0 -> x7, waiting for transfers between devices: none -> 14.1 us  [the longest x4 14.1 us: match_spans(): lax.ppermute(reply[-1] if reply else local_values, along_axis, by_rank)]
    psum x1, waiting for transfers between devices: 60.5 us -> 47.6 us  [on_device(): input_grad = lax.psum(d_entry_part, 'tensor') + spread(d_res_one)]
    psum x1, waiting for transfers between devices: 78 us -> 88.2 us  [on_device(): down_sum = lax.psum(down_part, 'tensor')]
    ppermute x0 -> x7, starting transfers between devices: none -> 10 us  [the longest x3 8.55 us: match_spans(): lax.ppermute(later[-1] if later else local_values, along_axis, gallery)]
  transfers between devices with their start and end apart: 11 -> 17, of which waited for: 11 -> 11; matrix products, arithmetic and copies ran while one was open for 8% -> 13% of each run, Pallas kernels for 0% -> 0%
where the time goes in v1:
time: 833 us; the launch traced here: 824 us
  waiting for transfers between devices  512 us (61%)
  matrix products  88.8 us (11%)
  blocking collectives  80.9 us (10%)
  local copies, waits for them, and re-layouts  61.8 us (7%)
  other arithmetic  52.1 us (6%)
  between operations  17.3 us (2%)
  starting transfers between devices  11.4 us (1%)
    reduce_scatter x4, waiting for transfers between devices, on_device(): lax.psum_scatter(part, 'dp', scatter_dimension=0, tiled=True)  177 us
    psum x1, waiting for transfers between devices, on_device(): attn_sum = lax.psum(attn_part, 'tensor')  96.1 us
    psum x1, waiting for transfers between devices, on_device(): down_sum = lax.psum(down_part, 'tensor')  88.2 us
    all_gather x1, waiting for transfers between devices, on_device(): lax.all_gather(change_rows[3], 'dp', axis=0, tiled=True)  52.9 us
    psum x1, waiting for transfers between devices, on_device(): input_grad = lax.psum(d_entry_part, 'tensor') + spread(d_res_one)  47.6 us
    psum x1, blocking collectives, on_device(): lax.psum((grad_gains, grad_biases, grad_bias_in), ('dp', 'tensor'))  40.8 us
    all_gather x1, blocking collectives, on_device(): lax.all_gather(change_rows[1], 'dp', axis=0, tiled=True)  40.1 us
    unnamed x90, local copies, waits for them, and re-layouts  22.3 us
  transfers between devices with their start and end apart: 17, of which 11 were waited for; matrix products, arithmetic and copies ran while one was open for 13% of the time, Pallas kernels for 0%

profile of v1, /device:TPU:0, one launch (start us, length us, event | category | flops | bytes accessed | tf_op | source)
XLA Modules:
  0.0 824.3 jit_solution(11945936480373938057)
XLA Ops:
  7.2 3.9 fusion.15
  14.5 2.1 convert_element_type.129
  18.9 2.5 fusion.170
  24.7 2.8 add_reduce_fusion
  36.0 5.7 fusion.20
  42.7 3.0 fusion.96
  46.6 96.1 %all-reduce.6.cloned.1.call-done = f32[1536,768]{1,0:T(8,128)} async-done(((f32[1536,768]{1,0:T(8,128)}), f32[1536,768]{1,0:T(8,128)}) %all-reduce.6.cloned.1.call-update) | async-done | bytes 4718608 | tf_op jit(solution)/shard_map/psum | solution.py:110
  142.6 3.8 fusion.169
  148.6 2.1 fusion.14
  150.6 17.8 %fusion.18 = f32[1536,768]{1,0:T(8,128)} fusion(bf16[1536,768]{1,0:T(8,128)(2,1)} %fusion.14, f32[768]{0:T(1024)S(1)} %dynamic_slice.23, f32[768,768]{1,0:T(8,128)} %param.31, f32[768,768]{1,0:T(8,128)} %param.30), kind=kOutput, calls=%fused_computation.40 | convolution fusion | flops 3702915072 | bytes 11799552 | tf_op jit(solution)/shard_map/tf,df->td/dot_general | solution.py:116
  169.4 2.2 fusion.58
  171.6 3.0 convolution_add_fusion.1
  174.6 88.2 %all-reduce.8.cloned.1.call-done = f32[1536,768]{1,0:T(8,128)} async-done(((f32[1536,768]{1,0:T(8,128)}), f32[1536,768]{1,0:T(8,128)}) %all-reduce.8.cloned.1.call-update) | async-done | bytes 4718608 | tf_op jit(solution)/shard_map/psum | solution.py:117
  262.8 4.7 fusion.168
  267.5 2.2 copy-done.4
  269.7 2.1 fusion.176
  271.9 2.0 multiply_reduce_fusion.8
  277.1 4.8 fusion.182
  284.1 3.0 fusion.89
  289.0 2.1 fusion.35
  292.9 4.5 fusion.175
  297.4 4.6 fusion.62
  303.0 15.6 %all-reduce.10.cloned.1.call-done = f32[240,768]{1,0:T(8,128)} async-done(((f32[240,768]{1,0:T(8,128)}), f32[240,768]{1,0:T(8,128)}) %all-reduce.10.cloned.1.call-update) | async-done | bytes 737296 | tf_op jit(solution)/shard_map/psum | solution.py:161
  325.7 2.5 stack_reshape.11
  339.4 4.4 fusion.183
  343.8 3.0 copy.96
  348.5 6.1 convolution_bitcast_fusion
  360.5 31.2 %reduce-scatter.9.cloned.1.call-done = f32[96,768]{1,0:T(8,128)} async-done(((f32[768,768]{1,0:T(8,128)}), f32[96,768]{1,0:T(8,128)}) %reduce-scatter.9.cloned.1.call-update) | async-done | bytes 294928 | tf_op jit(solution)/shard_map/reduce_scatter | solution.py:237
  391.7 2.2 fusion.105
  394.5 3.0 multiply_reduce_fusion
  397.5 3.9 add_convert_fusion
  402.1 40.8 %all-reduce = (f32[2,768]{1,0:T(2,128)S(1)}, f32[6,768]{1,0:T(8,128)S(1)}, f32[3072]{0:T(1024)S(1)}) all-reduce(f32[2,768]{1,0:T(2,128)S(1)} %maximum_multiply_fusion, f32[6,768]{1,0:T(8,128)S(1)} %stack.124, f32[3072]{0:T(1024)S(1)} %dynamic_update_slice.13), channel_id=1, replica_groups=mesh['dp'=8,'tensor'=4] {'dp','tensor'}, use_global_device_ids=true, to_apply=%region_27.28 | all-reduce | flops 9216 | bytes 73728 | tf_op jit(solution)/shard_map/psum | solution.py:230
  445.4 4.3 fusion.47
  449.7 13.9 %reduce-scatter.11.cloned.1.call-done = f32[96,768]{1,0:T(8,128)} async-done(((f32[768,768]{1,0:T(8,128)}), f32[96,768]{1,0:T(8,128)}) %reduce-scatter.11.cloned.1.call-update) | async-done | bytes 294928 | tf_op jit(solution)/shard_map/reduce_scatter | solution.py:237
  466.9 68.7 %reduce-scatter.5.cloned.1.call-done = f32[96,3,192]{2,0,1:T(8,128)} async-done(((f32[768,3,192]{2,0,1:T(8,128)}), f32[96,3,192]{2,0,1:T(8,128)}) %reduce-scatter.5.cloned.1.call-update) | async-done | bytes 221200 | tf_op jit(solution)/shard_map/reduce_scatter | solution.py:237
  537.8 63.3 %reduce-scatter.7.cloned.1.call-done = f32[96,192]{1,0:T(8,128)} async-done(((f32[768,192]{1,0:T(8,128)}), f32[96,192]{1,0:T(8,128)}) %reduce-scatter.7.cloned.1.call-update) | async-done | bytes 73744 | tf_op jit(solution)/shard_map/reduce_scatter | solution.py:237
  602.1 2.3 collective-permute-start.4
  604.5 40.1 %all_gather.9 = f32[768,192]{1,0:T(8,128)S(1)} all-gather(f32[96,192]{1,0:T(8,128)S(1)} %get-tuple-element.107), channel_id=1, replica_groups=mesh['dp'=8,'tensor'=4] {'dp'}, dimensions={0}, use_global_device_ids=true | all-gather | bytes 663552 | tf_op jit(solution)/shard_map/all_gather | solution.py:285
  649.0 47.6 %all-reduce.12.cloned.1.call-done = f32[1536,768]{1,0:T(8,128)} async-done(((f32[1536,768]{1,0:T(8,128)}), f32[1536,768]{1,0:T(8,128)}) %all-reduce.12.cloned.1.call-update) | async-done | bytes 4718608 | tf_op jit(solution)/shard_map/psum | solution.py:209
  696.6 6.6 bitcast_add_fusion
  704.1 4.2 collective-permute-start.6
  710.0 14.1 %collective-permute-done.3 = f32[96,3,192]{2,0,1:T(8,128)S(1)} collective-permute-done((f32[96,3,192]{2,0,1:T(8,128)S(1)}, f32[96,3,192]{2,0,1:T(8,128)S(1)}, u32[]{:S(2)}, u32[]{:S(2)}) %collective-permute-start.3) | collective-permute-done | bytes 221216 | tf_op jit(solution)/shard_map/ppermute | solution.py:271
  731.9 2.5 gather_fusion
  734.4 2.1 copy.98
  736.4 3.0 reshape.515
  739.4 20.2 %all-gather.3.cloned.1.call-done = f32[768,768]{1,0:T(8,128)} async-done(((f32[96,768]{1,0:T(8,128)}), f32[768,768]{1,0:T(8,128)}) %all-gather.3.cloned.1.call-update) | async-done | bytes 2359312 | tf_op jit(solution)/shard_map/all_gather | solution.py:286
  759.6 52.9 %all-gather.5.cloned.1.call-done = f32[768,768]{1,0:T(8,128)} async-done(((f32[96,768]{1,0:T(8,128)}), f32[768,768]{1,0:T(8,128)}) %all-gather.5.cloned.1.call-update) | async-done | bytes 2359312 | tf_op jit(solution)/shard_map/all_gather | solution.py:287
  812.5 3.4 copy.187
  (224 shorter events, 82.0 us)
Async XLA Ops:
  7.2 264.7 %copy-start = (bf16[1536,768]{1,0:T(8,128)(2,1)S(1)}, bf16[1536,768]{1,0:T(8,128)(2,1)}, u32[]{:S(2)}) copy-start(bf16[1536,768]{1,0:T(8,128)(2,1)} %param.22) | copy-start | bytes 7077892
  7.2 135.4 %all-reduce.6.cloned.1.call-start = ((), (), s32[]{:S(2)}) async-start(), calls=%async_computation.4 | async-start | bytes 9437184 | tf_op jit(solution)/shard_map/psum | solution.py:110
  11.2 2.1 copy-start.23
  11.2 3.3 copy-start.35
  13.2 14.2 %copy-start.7 = (f32[1536,1,192]{0,2,1:T(8,128)}, f32[1536,1,192]{0,2,1:T(8,128)S(1)}, u32[]{:S(2)}) copy-start(f32[1536,1,192]{0,2,1:T(8,128)S(1)} %get-tuple-element.95) | copy-start | bytes 3538948
  27.5 3.6 copy-start.3
  27.5 4.2 copy-start.11
  36.0 5.7 copy-start.14
  36.0 6.7 copy-start.18
  45.7 96.9 %copy-start.29 = (f32[768]{0:T(1024)S(1)}, f32[768]{0:T(1024)}, u32[]{:S(2)}) copy-start(f32[768]{0:T(1024)} %get-tuple-element.117) | copy-start | bytes 9220
  45.8 217.0 %all-reduce.8.cloned.1.call-start = ((), (), s32[]{:S(2)}) async-start(), calls=%async_computation.5 | async-start | bytes 9437184 | tf_op jit(solution)/shard_map/psum | solution.py:117
  146.4 2.1 copy-start.2
  168.4 94.4 %copy-start.31 = (f32[768]{0:T(1024)S(1)}, f32[768]{0:T(1024)}, u32[]{:S(2)}) copy-start(f32[768]{0:T(1024)} %get-tuple-element.119) | copy-start | bytes 9220
  168.4 150.1 %all-reduce.10.cloned.1.call-start = ((), (), s32[]{:S(2)}) async-start(), calls=%async_computation.6 | async-start | bytes 1474560 | tf_op jit(solution)/shard_map/psum | solution.py:161
  267.5 2.2 copy-start.4
  277.1 4.8 copy-start.15
  277.1 5.5 copy-start.6
  284.0 3.2 copy-start.8
  284.0 5.0 copy-start.37
  284.1 7.0 copy-start.10
  284.1 107.6 %reduce-scatter.9.cloned.1.call-start = ((), (), s32[]{:S(2)}) async-start(), calls=%async_computation.10 | async-start | bytes 2654208 | tf_op jit(solution)/shard_map/reduce_scatter | solution.py:237
  287.2 176.4 %reduce-scatter.11.cloned.1.call-start = ((), (), s32[]{:S(2)}) async-start(), calls=%async_computation.12 | async-start | bytes 2654208 | tf_op jit(solution)/shard_map/reduce_scatter | solution.py:237
  289.0 8.3 %copy-start.16 = (f32[240,768]{1,0:T(8,128)S(1)}, f32[240,768]{1,0:T(8,128)}, u32[]{:S(2)}) copy-start(f32[240,768]{1,0:T(8,128)} %copy-done.15) | copy-start | bytes 2211844
  301.9 233.7 %reduce-scatter.5.cloned.1.call-start = ((), (), s32[]{:S(2)}) async-start(), calls=%async_computation.8 | async-start | bytes 2654208 | tf_op jit(solution)/shard_map/reduce_scatter | solution.py:237
  320.8 7.4 copy-start.9
  331.1 6.9 copy-start.20
  343.8 3.1 copy-start.13
  346.9 254.2 %reduce-scatter.7.cloned.1.call-start = ((), (), s32[]{:S(2)}) async-start(), calls=%async_computation.9 | async-start | bytes 884736 | tf_op jit(solution)/shard_map/reduce_scatter | solution.py:237
  348.5 348.2 %all-reduce.12.cloned.1.call-start = ((), (), s32[]{:S(2)}) async-start(), calls=%async_computation.7 | async-start | bytes 9437184 | tf_op jit(solution)/shard_map/psum | solution.py:209
  354.6 5.4 copy-start.25
  354.6 5.5 copy-start.26
  354.6 5.5 copy-start.5
  354.6 39.5 %copy-start.30 = (f32[768]{0:T(1024)S(1)}, f32[768]{0:T(1024)}, u32[]{:S(2)}) copy-start(f32[768]{0:T(1024)} %get-tuple-element.70) | copy-start | bytes 9220
  354.6 39.6 %copy-start.34 = (f32[768]{0:T(1024)S(1)}, f32[768]{0:T(1024)}, u32[]{:S(2)}) copy-start(f32[768]{0:T(1024)} %get-tuple-element.146) | copy-start | bytes 9220
  354.7 404.9 %all-gather.3.cloned.1.call-start = ((), (), s32[]{:S(2)}) async-start(), calls=%async_computation.11 | async-start | bytes 2654208 | tf_op jit(solution)/shard_map/all_gather | solution.py:286
  393.9 418.6 %all-gather.5.cloned.1.call-start = ((), (), s32[]{:S(2)}) async-start(), calls=%async_computation.13 | async-start | bytes 2654208 | tf_op jit(solution)/shard_map/all_gather | solution.py:287
  397.5 45.4 %copy-start.24 = (f32[6,768]{1,0:T(8,128)S(1)}, f32[6,768]{1,0:T(8,128)}, u32[]{:S(2)}) copy-start(f32[6,768]{1,0:T(8,128)} %param.33) | copy-start | bytes 55300
  397.5 46.0 %copy-start.32 = (f32[2,2,768]{2,1,0:T(2,128)S(1)}, f32[2,2,768]{2,1,0:T(2,128)}, u32[]{:S(2)}) copy-start(f32[2,2,768]{2,1,0:T(2,128)} %param.39) | copy-start | bytes 36868
  401.4 62.2 %copy-start.22 = (f32[2,96,768]{2,1,0:T(8,128)S(1)}, f32[2,96,768]{2,1,0:T(8,128)}, u32[]{:S(2)}) copy-start(f32[2,96,768]{2,1,0:T(8,128)} %param.38) | copy-start | bytes 1769476
  537.0 67.5 %collective-permute-start = (f32[96,3,192]{2,0,1:T(8,128)S(1)}, f32[96,3,192]{2,0,1:T(8,128)S(1)}, u32[]{:S(2)}, u32[]{:S(2)}) collective-permute-start(f32[96,3,192]{2,0,1:T(8,128)S(1)} %get-tuple-element.104), channel_id=1, source_target_pairs={{0,4},{4,8},{8,12},{12,16},{16,20},{20,24},{24,28},{28,0},{1,5},{5... | collective-permute-start | bytes 663560 | tf_op jit(solution)/shard_map/ppermute | solution.py:271
  602.1 44.2 %collective-permute-start.4 = (f32[96,3,192]{2,0,1:T(8,128)S(1)}, f32[96,3,192]{2,0,1:T(8,128)}, u32[]{:S(2)}, u32[]{:S(2)}) collective-permute-start(f32[96,3,192]{2,0,1:T(8,128)S(1)} %get-tuple-element.104), channel_id=1, source_target_pairs={{4,0},{8,4},{12,8},{16,12},{20,16},{24,20},{28,24},{0,28},{5,1},{9... | collective-permute-start | bytes 663560 | tf_op jit(solution)/shard_map/ppermute | solution.py:275
  604.5 43.9 %collective-permute-start.1 = (f32[96,3,192]{2,0,1:T(8,128)S(1)}, f32[96,3,192]{2,0,1:T(8,128)}, u32[]{:S(2)}, u32[]{:S(2)}) collective-permute-start(f32[96,3,192]{2,0,1:T(8,128)S(1)} %collective-permute-done), channel_id=1, source_target_pairs={{0,4},{4,8},{8,12},{12,16},{16,20},{20,24},{24,28},{28,0},{1,5},{5... | collective-permute-start | bytes 663560 | tf_op jit(solution)/shard_map/ppermute | solution.py:271
  646.4 57.7 %collective-permute-start.5 = (f32[96,3,192]{2,0,1:T(8,128)}, f32[96,3,192]{2,0,1:T(8,128)S(1)}, u32[]{:S(2)}, u32[]{:S(2)}) collective-permute-start(f32[96,3,192]{2,0,1:T(8,128)} %collective-permute-done.4), channel_id=1, source_target_pairs={{4,0},{8,4},{12,8},{16,12},{20,16},{24,20},{28,24},{0,28},{5,1},{9... | collective-permute-start | bytes 663560 | tf_op jit(solution)/shard_map/ppermute | solution.py:275
  648.4 59.9 %collective-permute-start.2 = (f32[96,3,192]{2,0,1:T(8,128)}, f32[96,3,192]{2,0,1:T(8,128)S(1)}, u32[]{:S(2)}, u32[]{:S(2)}) collective-permute-start(f32[96,3,192]{2,0,1:T(8,128)} %collective-permute-done.1), channel_id=1, source_target_pairs={{0,4},{4,8},{8,12},{12,16},{16,20},{20,24},{24,28},{28,0},{1,5},{5... | collective-permute-start | bytes 663560 | tf_op jit(solution)/shard_map/ppermute | solution.py:271
  704.1 27.1 %collective-permute-start.6 = (f32[96,3,192]{2,0,1:T(8,128)S(1)}, f32[96,3,192]{2,0,1:T(8,128)S(1)}, u32[]{:S(2)}, u32[]{:S(2)}) collective-permute-start(f32[96,3,192]{2,0,1:T(8,128)S(1)} %collective-permute-done.5), channel_id=1, source_target_pairs={{4,0},{8,4},{12,8},{16,12},{20,16},{24,20},{28,24},{0,28},{5,1},{9... | collective-permute-start | bytes 663560 | tf_op jit(solution)/shard_map/ppermute | solution.py:275
  708.3 15.8 %collective-permute-start.3 = (f32[96,3,192]{2,0,1:T(8,128)S(1)}, f32[96,3,192]{2,0,1:T(8,128)S(1)}, u32[]{:S(2)}, u32[]{:S(2)}) collective-permute-start(f32[96,3,192]{2,0,1:T(8,128)S(1)} %collective-permute-done.2), channel_id=1, source_target_pairs={{0,4},{4,8},{8,12},{12,16},{16,20},{20,24},{24,28},{28,0},{1,5},{5... | collective-permute-start | bytes 663560 | tf_op jit(solution)/shard_map/ppermute | solution.py:271
  812.5 3.4 copy-start.19
  812.5 4.8 copy-start.1
  (7 other events, 5.3 us)
Sparse Core Ops, SparseCore 0:
  45.9 96.7 all-reduce.5
  168.6 94.1 all-reduce.7
  284.2 34.3 all-reduce.9
  322.5 69.1 reduce-scatter.8
  395.1 68.5 reduce-scatter.10
  467.5 68.0 reduce-scatter.4
  539.5 61.5 reduce-scatter.6
  603.6 93.0 all-reduce.11
  699.6 59.8 all-gather.2
  761.8 50.6 all-gather.4
